TPU v7x, 32 devices: a whole 2x2x4 slice. The times are simulated.
32 devices in a mesh: member: 2 (over core), tile: 16 (over z, y, x).
Axes of the slice: x: 2, y: 2, z: 4, core: 2. Of those that a mesh axis runs over, the one named last changes fastest.
Arguments:
- member_predictions: bfloat16 [4, 80, 768, 1536], P(None, 'member', 'tile'), may hold values from -5 to 13
- meridional_operator: float32 [384, 128], replicated, may hold values from -0.3125 to 0.3125
- zonal_operator: float32 [256, 48], P('tile'), may hold values from -0.875 to 0.875
Outputs:
- coarse_anomalies: float32 [4, 80, 512, 256], P(None, None, 'tile', 'member')
All inputs are finite; a program needn't handle non-finite values.
Results may differ from a plain program's by a relative error of at most 0.0003.
Values sent between devices are 32-bit elements; how exact they have to be, the bound alone decides.
A program may use at most 128 MiB of HBM per device.

v0:
```python
import functools
import math

import jax
import jax.numpy as jnp
from jax import lax
from jax.experimental import pallas as pl
from jax.experimental.pallas import tpu as pltpu
from jax.sharding import PartitionSpec as P

MESH = pl.DeviceIdType.MESH
PACK = 8
DEPTH = 3


def two_parts(value):
    high = value.astype(jnp.bfloat16)
    low = (value - high.astype(jnp.float32)).astype(jnp.bfloat16)
    return high, low


def three_parts(value):
    high = value.astype(jnp.bfloat16)
    rest = value - high.astype(jnp.float32)
    middle = rest.astype(jnp.bfloat16)
    low = (rest - middle.astype(jnp.float32)).astype(jnp.bfloat16)
    return high, middle, low


def piece_index(shape, dimension, size):
    at = lax.broadcasted_iota(jnp.int32, shape, dimension)
    piece = jnp.zeros(shape, jnp.int32)
    for f in range(1, PACK):
        piece = piece + jnp.where(at >= f * size, 1, 0)
    return piece


def block_diagonal(part, width):
    coarse = part.shape[0]
    row_piece = piece_index((PACK * coarse, 1), 0, coarse)
    col_piece = piece_index((1, PACK * width), 1, width)
    within = lax.broadcasted_iota(jnp.int32, (1, PACK * width), 1) - col_piece * width
    spread = lax.broadcasted_iota(jnp.int32, (width, PACK * width), 0) == within
    spread = jnp.where(spread, 1.0, 0.0).astype(jnp.bfloat16)
    wide = jnp.dot(part, spread, preferred_element_type=jnp.float32)
    tall = jnp.concatenate([wide] * PACK, axis=0)
    return jnp.where(row_piece == col_piece, tall, 0.0).astype(jnp.bfloat16)


def swap_pieces(blocks, piece):
    lanes = blocks[0].shape[-1]
    lane = lax.broadcasted_iota(jnp.int32, blocks[0].shape, blocks[0].ndim - 1)
    axis = blocks[0].ndim - 1
    blocks = list(blocks)
    d = PACK // 2
    while d >= 1:
        shift = d * piece
        upper = (lane & shift) != 0
        for s in range(PACK):
            if s & d:
                continue
            a, b = blocks[s], blocks[s + d]
            if 2 * shift == lanes:
                both = pltpu.roll(jnp.where(upper, a, b), shift, axis)
                blocks[s] = jnp.where(upper, both, a)
                blocks[s + d] = jnp.where(upper, b, both)
            else:
                blocks[s] = jnp.where(upper, pltpu.roll(b, shift, axis), a)
                blocks[s + d] = jnp.where(upper, b, pltpu.roll(a, lanes - shift, axis))
        d //= 2
    return blocks


def exchange_kernel(
    members,
    tiles,
    block,
    x_ref,
    op_ref,
    raw_ref,
    mean_ref,
    xbuf,
    zon2,
    mer2,
    across_ref,
    sendbuf,
    got_ref,
    first_ref,
    x_sem,
    first_send_sem,
    first_recv_sem,
    short_sem,
    send_sem,
    recv_sem,
    own_sem,
):
    levels, local, width, fine = x_ref.shape
    per_block = op_ref.shape[1]
    groups, rows, lanes = sendbuf.shape[1:]
    per = PACK // levels
    spread = tiles // members
    bands = fine // block
    tiles_per_band = tiles // bands
    count = members * local
    piece = lanes // PACK
    packed = per == 2 and rows % 16 == 0
    me = lax.axis_index("member")
    tile = lax.axis_index("tile")
    target = tile // spread
    slot_there = me * spread + lax.rem(tile, spread)
    stays = target == me
    side = tile // (tiles // 2)

    def fetch(g, slot):
        return pltpu.make_async_copy(x_ref.at[:, pl.ds(g * per, per)], xbuf.at[slot], x_sem.at[slot])

    fetch(0, 0).start()

    barrier = pltpu.get_barrier_semaphore()
    for h in range(members):
        for s in range(spread):
            source = me * spread + s

            @pl.when(jnp.logical_not((h == me) & (source == tile)))
            def _():
                pl.semaphore_signal(barrier, inc=1, device_id=(h, source), device_id_type=MESH)

    @pl.when(me != 0)
    def _():
        pl.semaphore_signal(barrier, inc=1, device_id=(0, tile), device_id_type=MESH)

    zon_high, zon_low = two_parts(op_ref[block : block + piece, :width])
    zon2[:lanes] = block_diagonal(zon_high, width)
    zon2[lanes:] = block_diagonal(zon_low, width)
    mer_high, mer_low = two_parts(op_ref[:block].T)
    mer2[:per_block] = mer_high
    mer2[per_block:] = mer_low
    for g in range(1, min(DEPTH, groups)):
        fetch(g, g).start()

    def remote(there, g, short=False):
        height = pl.ds(0, rows // 2 if short else rows)
        return pltpu.make_async_remote_copy(
            src_ref=sendbuf.at[there, g, height],
            dst_ref=got_ref.at[slot_there, g, height],
            send_sem=(short_sem if isinstance(g, int) else send_sem).at[there],
            recv_sem=recv_sem.at[slot_there, g],
            device_id=(target, there),
            device_id_type=MESH,
        )

    def first_copy(h, j, where):
        return pltpu.make_async_remote_copy(
            src_ref=first_ref.at[where],
            dst_ref=first_ref.at[where],
            send_sem=first_send_sem.at[h, j],
            recv_sem=first_recv_sem.at[j],
            device_id=(h, tile),
            device_id_type=MESH,
        )

    turn = lax.rem(piece_index((1, lanes), 1, piece), per)

    def step(g, _):
        slot = g % DEPTH if isinstance(g, int) else lax.rem(g, DEPTH)
        fetch(g, slot).wait()
        fields = xbuf[slot].reshape(PACK * width, fine)
        across = jnp.dot(zon2[...], fields, preferred_element_type=jnp.float32)
        across_ref[...] = across[lanes:] + across[:lanes]
        for j in range(bands):
            band = lax.rem((1 - side) * (bands // 2) + j, bands)
            first = band * tiles_per_band
            high, middle, low = three_parts(across_ref[:, pl.ds(pl.multiple_of(band * block, block), block)])
            parts = jnp.concatenate([high, middle, low], axis=0)
            out = lax.dot_general(
                mer2[...], parts, (((1,), (1,)), ((), ())), preferred_element_type=jnp.float32
            )
            top, bottom = out[:per_block], out[per_block:]
            total = top[:, 2 * lanes :] + bottom[:, lanes : 2 * lanes]
            total = total + top[:, lanes : 2 * lanes] + bottom[:, :lanes]
            total = total + top[:, :lanes]
            where = pl.ds(pl.multiple_of(band * per_block, per_block), per_block)
            begins = isinstance(g, int)
            if begins:

                @pl.when(me == 0)
                def _():
                    kept = total
                    for m in range(1, per):
                        kept = jnp.where(turn == m, pltpu.roll(total, m * piece, 1), kept)
                    first_ref[where] = kept

                if j == 0:
                    extra = jnp.where(me == 0, members - 1, 0)
                    pl.semaphore_wait(barrier, tiles - jnp.where(stays, 1, 0) + extra)

                @pl.when(me == 0)
                def _():
                    for h in range(1, members):
                        first_copy(h, j, where).start()

                @pl.when(me != 0)
                def _():
                    first_copy(0, j, where).wait_recv()

            total = total - first_ref[where]
            for q in range(tiles_per_band):
                sendbuf[first + q, g] = total[q * rows : (q + 1) * rows]
            if begins and packed:

                @pl.when(me == 0)
                def _():
                    for q in range(tiles_per_band):
                        top = total[q * rows : q * rows + rows // 2]
                        bottom = total[q * rows + rows // 2 : (q + 1) * rows]
                        both = jnp.where(turn == 1, top, pltpu.roll(bottom, lanes - piece, 1))
                        sendbuf[first + q, g, : rows // 2] = both

            for q in range(tiles_per_band):
                there = first + lax.rem(tile + q, tiles_per_band)
                away = None
                if q == 0 and j >= bands // 2:
                    own = stays & (there == tile)
                    away = jnp.logical_not(own)

                    @pl.when(own)
                    def _():
                        pltpu.make_async_copy(sendbuf.at[tile, g], got_ref.at[slot_there, g], own_sem).start()

                if begins and packed:
                    low_end = me == 0 if away is None else (me == 0) & away
                    other = me != 0 if away is None else (me != 0) & away

                    @pl.when(low_end)
                    def _():
                        remote(there, g, True).start()

                    @pl.when(other)
                    def _():
                        remote(there, g).start()

                elif away is not None:

                    @pl.when(away)
                    def _():
                        remote(there, g).start()

                else:
                    remote(there, g).start()

        @pl.when(jnp.asarray(g + DEPTH < groups))
        def _():
            fetch(g + DEPTH, slot).start()

        return 0

    step(0, 0)
    lax.fori_loop(1, groups, step, 0)

    @pl.when(stays)
    def _():
        pltpu.make_async_copy(sendbuf.at[tile], got_ref.at[slot_there], own_sem).wait()

    mean_ref[...] = jnp.zeros_like(mean_ref)

    def arrival(g, _):
        for h in range(members):
            short = packed and isinstance(g, int) and h == 0
            height = rows // 2 if short else rows
            for slot in range(h * spread, (h + 1) * spread):

                @pl.when(jnp.logical_not(stays & (slot_there == slot)))
                def _():
                    pltpu.make_async_remote_copy(
                        src_ref=sendbuf.at[0, g, pl.ds(0, height)],
                        dst_ref=got_ref.at[slot, g, pl.ds(0, height)],
                        send_sem=send_sem.at[0],
                        recv_sem=recv_sem.at[slot, g],
                        device_id=(target, 0),
                        device_id_type=MESH,
                    ).wait_recv()

            for part in range(spread // PACK):
                base = h * spread + part * PACK
                columns = slice(part * lanes, (part + 1) * lanes)
                blocks = [got_ref[base + s, g, :height] for s in range(PACK)]
                if short:
                    blocks = [
                        jnp.concatenate(
                            [jnp.where(turn == 1, both, 0.0), jnp.where(turn == 1, pltpu.roll(both, piece, 1), 0.0)],
                            axis=0,
                        )
                        for both in blocks
                    ]
                fields = swap_pieces(blocks, piece)
                for f in range(PACK):
                    raw_ref[f // per, h * local + g * per + f % per, :, columns] = fields[f]
                for level in range(levels):
                    total = fields[level * per]
                    for m in range(1, per):
                        total = total + fields[level * per + m]
                    mean_ref[level, :, columns] += total
        return 0

    arrival(0, 0)
    lax.fori_loop(1, groups - 1, arrival, 0)
    for there in range(tiles):

        @pl.when(jnp.logical_not(stays & (tile == there)))
        def _():
            rest = pl.ds(1, groups - 1)
            pltpu.make_async_remote_copy(
                src_ref=sendbuf.at[there, rest],
                dst_ref=got_ref.at[slot_there, rest],
                send_sem=send_sem.at[there],
                recv_sem=recv_sem.at[slot_there, 0],
                device_id=(target, there),
                device_id_type=MESH,
            ).wait_send()
            if packed:

                @pl.when(me == 0)
                def _():
                    remote(there, 0, True).wait_send()

                @pl.when(me != 0)
                def _():
                    remote(there, 0).wait_send()

            else:
                remote(there, 0).wait_send()

    @pl.when(me == 0)
    def _():
        for h in range(1, members):
            for j in range(bands):
                first_copy(h, j, pl.ds(j * per_block, per_block)).wait_send()

    lax.fori_loop(groups - 1, groups, arrival, 0)
    mean_ref[...] = mean_ref[...] / count


def center_kernel(chunk, raw_ref, mean_ref, out_ref, outbuf, sem):
    levels, count = raw_ref.shape[:2]
    scale = 1.0 / math.sqrt(count - 1)
    for level in range(levels):
        mean = mean_ref[level]
        for start in range(0, count, chunk):

            def center(m, _, start=start, level=level, mean=mean):
                outbuf[level, start + m] = (raw_ref[level, start + m] - mean) * scale
                return 0

            lax.fori_loop(0, chunk, center, 0, unroll=5)
            at = pl.ds(start, chunk)
            pltpu.make_async_copy(outbuf.at[level, at], out_ref.at[level, at], sem).start()
    pltpu.make_async_copy(outbuf, out_ref, sem).wait()


def body(members, tiles, x, meridional, zonal):
    levels, local, width, fine = x.shape
    block, per_block = meridional.shape
    coarse = zonal.shape[0]
    lanes = PACK * coarse
    groups = levels * local // PACK
    rows = fine // block * per_block // tiles
    spread = tiles // members
    assert PACK % levels == 0 and local % (PACK // levels) == 0 and spread % PACK == 0 and per_block % rows == 0
    assert fine // block % 2 == 0
    anywhere = pl.BlockSpec(memory_space=pl.ANY)
    count = local * members
    columns = spread * coarse
    operators = jnp.concatenate([meridional, jnp.pad(zonal, ((0, 0), (0, per_block - width)))], axis=0)
    raw, mean = pl.pallas_call(
        functools.partial(exchange_kernel, members, tiles, block),
        out_shape=[
            jax.ShapeDtypeStruct((levels, count, rows, columns), jnp.float32),
            jax.ShapeDtypeStruct((levels, rows, columns), jnp.float32),
        ],
        in_specs=[anywhere, pl.BlockSpec(memory_space=pltpu.VMEM)],
        out_specs=[pl.BlockSpec(memory_space=pltpu.VMEM)] * 2,
        scratch_shapes=[
            pltpu.VMEM((DEPTH, levels, PACK // levels, width, fine), jnp.bfloat16),
            pltpu.VMEM((2 * lanes, PACK * width), jnp.bfloat16),
            pltpu.VMEM((2 * per_block, block), jnp.bfloat16),
            pltpu.VMEM((lanes, fine), jnp.float32),
            pltpu.VMEM((tiles, groups, rows, lanes), jnp.float32),
            pltpu.VMEM((tiles, groups, rows, lanes), jnp.float32),
            pltpu.VMEM((tiles * rows, lanes), jnp.float32),
            pltpu.SemaphoreType.DMA((DEPTH,)),
            pltpu.SemaphoreType.DMA((members, fine // block)),
            pltpu.SemaphoreType.DMA((fine // block,)),
            pltpu.SemaphoreType.DMA((tiles,)),
            pltpu.SemaphoreType.DMA((tiles,)),
            pltpu.SemaphoreType.DMA((tiles, groups)),
            pltpu.SemaphoreType.DMA,
        ],
        compiler_params=pltpu.CompilerParams(
            collective_id=0, has_side_effects=True, vmem_limit_bytes=40 * 1024 * 1024
        ),
        name="restrict_exchange",
    )(x, operators)
    return pl.pallas_call(
        functools.partial(center_kernel, 16 if count % 16 == 0 else count),
        out_shape=jax.ShapeDtypeStruct((levels, count, rows, columns), jnp.float32),
        in_specs=[pl.BlockSpec(memory_space=pltpu.VMEM)] * 2,
        out_specs=anywhere,
        scratch_shapes=[
            pltpu.VMEM((levels, count, rows, columns), jnp.float32),
            pltpu.SemaphoreType.DMA,
        ],
        compiler_params=pltpu.CompilerParams(vmem_limit_bytes=16 * 1024 * 1024),
        name="center_scale",
    )(raw, mean)


def solution(mesh):
    members, tiles = mesh.shape["member"], mesh.shape["tile"]
    return jax.shard_map(
        functools.partial(body, members, tiles),
        mesh=mesh,
        in_specs=(P(None, "member", "tile", None), P(), P("tile", None)),
        out_specs=P(None, None, "tile", "member"),
        check_vma=False,
    )
```

profile of v0, /device:TPU:1, one launch (start us, length us, event | category | flops | bytes accessed | tf_op | source)
XLA Modules:
  0.0 125.9 jit_solution(2307813727082643422)
XLA Ops:
  0.0 1.0 select_maximum_fusion.op_ref
  1.0 122.6 %restrict_exchange.1 = (f32[4,80,32,128]{3,2,1,0:T(8,128)S(1)}, f32[4,32,128]{2,1,0:T(8,128)S(1)}) custom-call(bf16[4,40,48,1536]{3,2,1,0:T(8,128)(2,1)} %x_ref.1, f32[400,128]{1,0:T(8,128)S(1)} %select_maximum_fusion.op_ref), custom_call_target="tpu_custom_call" | custom-call | tf_op jit(solution)/shard_map/restrict_exchange/pallas_call | solution.py:374
  123.6 2.4 %center_scale.1 = f32[4,80,32,128]{3,2,1,0:T(8,128)} custom-call(f32[4,80,32,128]{3,2,1,0:T(8,128)S(1)} %get-tuple-element.7.raw_ref, f32[4,32,128]{2,1,0:T(8,128)S(1)} %get-tuple-element.8.mean_ref), custom_call_target="tpu_custom_call" | custom-call | tf_op jit(solution)/shard_map/center_scale/pallas_call | solution.py:403
where the time goes:
time: 126 us
  Pallas kernels  125 us (99%)
    pallas_call x1, Pallas kernels, body(): pl.pallas_call(functools.partial(exchange_kernel, members, tiles, block),...  123 us

commit v1 on v0

--- a/solution.py
+++ b/solution.py
@@ -110,6 +110,9 @@
     slot_there = me * spread + lax.rem(tile, spread)
     stays = target == me
     side = tile // (tiles // 2)
+    quarter = tile // (tiles // 4)
+    outer = (quarter == 0) | (quarter == 3)
+    early = jnp.where(outer, 1 - side, side)
 
     def fetch(g, slot):
         return pltpu.make_async_copy(x_ref.at[:, pl.ds(g * per, per)], xbuf.at[slot], x_sem.at[slot])
@@ -161,6 +164,39 @@
 
     turn = lax.rem(piece_index((1, lanes), 1, piece), per)
 
+    def send(first, g):
+        for q in range(tiles_per_band):
+            there = first + lax.rem(tile + q, tiles_per_band)
+            away = None
+            if q == 0:
+                own = stays & (there == tile)
+                away = jnp.logical_not(own)
+
+                @pl.when(own)
+                def _():
+                    pltpu.make_async_copy(sendbuf.at[tile, g], got_ref.at[slot_there, g], own_sem).start()
+
+            if isinstance(g, int) and packed:
+                low_end = me == 0 if away is None else (me == 0) & away
+                other = me != 0 if away is None else (me != 0) & away
+
+                @pl.when(low_end)
+                def _():
+                    remote(there, g, True).start()
+
+                @pl.when(other)
+                def _():
+                    remote(there, g).start()
+
+            elif away is not None:
+
+                @pl.when(away)
+                def _():
+                    remote(there, g).start()
+
+            else:
+                remote(there, g).start()
+
     def step(g, _):
         slot = g % DEPTH if isinstance(g, int) else lax.rem(g, DEPTH)
         fetch(g, slot).wait()
@@ -168,7 +204,7 @@
         across = jnp.dot(zon2[...], fields, preferred_element_type=jnp.float32)
         across_ref[...] = across[lanes:] + across[:lanes]
         for j in range(bands):
-            band = lax.rem((1 - side) * (bands // 2) + j, bands)
+            band = lax.rem(early * (bands // 2) + j, bands)
             first = band * tiles_per_band
             high, middle, low = three_parts(across_ref[:, pl.ds(pl.multiple_of(band * block, block), block)])
             parts = jnp.concatenate([high, middle, low], axis=0)
@@ -216,37 +252,8 @@
                         both = jnp.where(turn == 1, top, pltpu.roll(bottom, lanes - piece, 1))
                         sendbuf[first + q, g, : rows // 2] = both
 
-            for q in range(tiles_per_band):
-                there = first + lax.rem(tile + q, tiles_per_band)
-                away = None
-                if q == 0 and j >= bands // 2:
-                    own = stays & (there == tile)
-                    away = jnp.logical_not(own)
-
-                    @pl.when(own)
-                    def _():
-                        pltpu.make_async_copy(sendbuf.at[tile, g], got_ref.at[slot_there, g], own_sem).start()
-
-                if begins and packed:
-                    low_end = me == 0 if away is None else (me == 0) & away
-                    other = me != 0 if away is None else (me != 0) & away
-
-                    @pl.when(low_end)
-                    def _():
-                        remote(there, g, True).start()
-
-                    @pl.when(other)
-                    def _():
-                        remote(there, g).start()
-
-                elif away is not None:
-
-                    @pl.when(away)
-                    def _():
-                        remote(there, g).start()
-
-                else:
-                    remote(there, g).start()
+            if j < bands // 2:
+                send(first, g)
 
         @pl.when(jnp.asarray(g + DEPTH < groups))
         def _():
@@ -254,8 +261,15 @@
 
         return 0
 
+    def later(g, _):
+        for j in range(bands // 2):
+            send(((1 - early) * (bands // 2) + j) * tiles_per_band, g)
+        return 0
+
     step(0, 0)
     lax.fori_loop(1, groups, step, 0)
+    later(0, 0)
+    lax.fori_loop(1, groups, later, 0)
 
     @pl.when(stays)
     def _():
@@ -366,7 +380,7 @@
     rows = fine // block * per_block // tiles
     spread = tiles // members
     assert PACK % levels == 0 and local % (PACK // levels) == 0 and spread % PACK == 0 and per_block % rows == 0
-    assert fine // block % 2 == 0
+    assert fine // block % 2 == 0 and tiles % 4 == 0
     anywhere = pl.BlockSpec(memory_space=pl.ANY)
     count = local * members
     columns = spread * coarse

time: 126 us -> 127 us (level)
  no operation moved by 1% of the time
where the time goes in v1:
time: 127 us
  Pallas kernels  126 us (99%)
    pallas_call x1, Pallas kernels, body(): pl.pallas_call(functools.partial(exchange_kernel, members, tiles, block),...  124 us

profile of v1, /device:TPU:1, one launch (start us, length us, event | category | flops | bytes accessed | tf_op | source)
XLA Modules:
  0.0 127.0 jit_solution(17278003759486384562)
XLA Ops:
  0.0 1.0 select_maximum_fusion.op_ref
  1.0 123.7 %restrict_exchange.1 = (f32[4,80,32,128]{3,2,1,0:T(8,128)S(1)}, f32[4,32,128]{2,1,0:T(8,128)S(1)}) custom-call(bf16[4,40,48,1536]{3,2,1,0:T(8,128)(2,1)} %x_ref.1, f32[400,128]{1,0:T(8,128)S(1)} %select_maximum_fusion.op_ref), custom_call_target="tpu_custom_call" | custom-call | tf_op jit(solution)/shard_map/restrict_exchange/pallas_call | solution.py:388
  124.7 2.4 %center_scale.1 = f32[4,80,32,128]{3,2,1,0:T(8,128)} custom-call(f32[4,80,32,128]{3,2,1,0:T(8,128)S(1)} %get-tuple-element.7.raw_ref, f32[4,32,128]{2,1,0:T(8,128)S(1)} %get-tuple-element.8.mean_ref), custom_call_target="tpu_custom_call" | custom-call | tf_op jit(solution)/shard_map/center_scale/pallas_call | solution.py:417

commit v2 on v0

--- a/solution.py
+++ b/solution.py
@@ -82,7 +82,6 @@
     xbuf,
     zon2,
     mer2,
-    across_ref,
     sendbuf,
     got_ref,
     first_ref,
@@ -164,13 +163,13 @@
     def step(g, _):
         slot = g % DEPTH if isinstance(g, int) else lax.rem(g, DEPTH)
         fetch(g, slot).wait()
-        fields = xbuf[slot].reshape(PACK * width, fine)
-        across = jnp.dot(zon2[...], fields, preferred_element_type=jnp.float32)
-        across_ref[...] = across[lanes:] + across[:lanes]
         for j in range(bands):
             band = lax.rem((1 - side) * (bands // 2) + j, bands)
             first = band * tiles_per_band
-            high, middle, low = three_parts(across_ref[:, pl.ds(pl.multiple_of(band * block, block), block)])
+            latitudes = pl.ds(pl.multiple_of(band * block, block), block)
+            fields = xbuf[slot, :, :, :, latitudes].reshape(PACK * width, block)
+            across = jnp.dot(zon2[...], fields, preferred_element_type=jnp.float32)
+            high, middle, low = three_parts(across[lanes:] + across[:lanes])
             parts = jnp.concatenate([high, middle, low], axis=0)
             out = lax.dot_general(
                 mer2[...], parts, (((1,), (1,)), ((), ())), preferred_element_type=jnp.float32
@@ -383,7 +382,6 @@
             pltpu.VMEM((DEPTH, levels, PACK // levels, width, fine), jnp.bfloat16),
             pltpu.VMEM((2 * lanes, PACK * width), jnp.bfloat16),
             pltpu.VMEM((2 * per_block, block), jnp.bfloat16),
-            pltpu.VMEM((lanes, fine), jnp.float32),
             pltpu.VMEM((tiles, groups, rows, lanes), jnp.float32),
             pltpu.VMEM((tiles, groups, rows, lanes), jnp.float32),
             pltpu.VMEM((tiles * rows, lanes), jnp.float32),

time: 126 us -> 126 us (level)
  no operation moved by 1% of the time
where the time goes in v2:
time: 126 us
  Pallas kernels  125 us (99%)
    pallas_call x1, Pallas kernels, body(): pl.pallas_call(functools.partial(exchange_kernel, members, tiles, block),...  122 us

profile of v2, /device:TPU:1, one launch (start us, length us, event | category | flops | bytes accessed | tf_op | source)
XLA Modules:
  0.0 125.5 jit_solution(2727312264035901339)
XLA Ops:
  0.0 1.0 select_maximum_fusion.op_ref
  1.0 122.2 %restrict_exchange.1 = (f32[4,80,32,128]{3,2,1,0:T(8,128)S(1)}, f32[4,32,128]{2,1,0:T(8,128)S(1)}) custom-call(bf16[4,40,48,1536]{3,2,1,0:T(8,128)(2,1)} %x_ref.1, f32[400,128]{1,0:T(8,128)S(1)} %select_maximum_fusion.op_ref), custom_call_target="tpu_custom_call" | custom-call | tf_op jit(solution)/shard_map/restrict_exchange/pallas_call | solution.py:373
  123.2 2.4 %center_scale.1 = f32[4,80,32,128]{3,2,1,0:T(8,128)} custom-call(f32[4,80,32,128]{3,2,1,0:T(8,128)S(1)} %get-tuple-element.7.raw_ref, f32[4,32,128]{2,1,0:T(8,128)S(1)} %get-tuple-element.8.mean_ref), custom_call_target="tpu_custom_call" | custom-call | tf_op jit(solution)/shard_map/center_scale/pallas_call | solution.py:401

commit v3 on v1

--- a/solution.py
+++ b/solution.py
@@ -82,7 +82,6 @@
     xbuf,
     zon2,
     mer2,
-    across_ref,
     sendbuf,
     got_ref,
     first_ref,
@@ -110,9 +109,6 @@
     slot_there = me * spread + lax.rem(tile, spread)
     stays = target == me
     side = tile // (tiles // 2)
-    quarter = tile // (tiles // 4)
-    outer = (quarter == 0) | (quarter == 3)
-    early = jnp.where(outer, 1 - side, side)
 
     def fetch(g, slot):
         return pltpu.make_async_copy(x_ref.at[:, pl.ds(g * per, per)], xbuf.at[slot], x_sem.at[slot])
@@ -164,9 +160,9 @@
 
     turn = lax.rem(piece_index((1, lanes), 1, piece), per)
 
-    def send(first, g):
-        for q in range(tiles_per_band):
-            there = first + lax.rem(tile + q, tiles_per_band)
+    def send(first, span, g):
+        for q in range(span):
+            there = first + lax.rem(tile + q, span)
             away = None
             if q == 0:
                 own = stays & (there == tile)
@@ -200,13 +196,13 @@
     def step(g, _):
         slot = g % DEPTH if isinstance(g, int) else lax.rem(g, DEPTH)
         fetch(g, slot).wait()
-        fields = xbuf[slot].reshape(PACK * width, fine)
-        across = jnp.dot(zon2[...], fields, preferred_element_type=jnp.float32)
-        across_ref[...] = across[lanes:] + across[:lanes]
         for j in range(bands):
-            band = lax.rem(early * (bands // 2) + j, bands)
+            band = lax.rem((1 - side) * (bands // 2) + j, bands)
             first = band * tiles_per_band
-            high, middle, low = three_parts(across_ref[:, pl.ds(pl.multiple_of(band * block, block), block)])
+            latitudes = pl.ds(pl.multiple_of(band * block, block), block)
+            fields = xbuf[slot, :, :, :, latitudes].reshape(PACK * width, block)
+            across = jnp.dot(zon2[...], fields, preferred_element_type=jnp.float32)
+            high, middle, low = three_parts(across[lanes:] + across[:lanes])
             parts = jnp.concatenate([high, middle, low], axis=0)
             out = lax.dot_general(
                 mer2[...], parts, (((1,), (1,)), ((), ())), preferred_element_type=jnp.float32
@@ -252,8 +248,11 @@
                         both = jnp.where(turn == 1, top, pltpu.roll(bottom, lanes - piece, 1))
                         sendbuf[first + q, g, : rows // 2] = both
 
-            if j < bands // 2:
-                send(first, g)
+            if begins:
+                send(first, tiles_per_band, g)
+            elif (j + 1) % (bands // 2) == 0:
+                far = 1 - side if j < bands // 2 else side
+                send(far * (tiles // 2), tiles // 2, g)
 
         @pl.when(jnp.asarray(g + DEPTH < groups))
         def _():
@@ -261,15 +260,8 @@
 
         return 0
 
-    def later(g, _):
-        for j in range(bands // 2):
-            send(((1 - early) * (bands // 2) + j) * tiles_per_band, g)
-        return 0
-
     step(0, 0)
     lax.fori_loop(1, groups, step, 0)
-    later(0, 0)
-    lax.fori_loop(1, groups, later, 0)
 
     @pl.when(stays)
     def _():
@@ -380,7 +372,7 @@
     rows = fine // block * per_block // tiles
     spread = tiles // members
     assert PACK % levels == 0 and local % (PACK // levels) == 0 and spread % PACK == 0 and per_block % rows == 0
-    assert fine // block % 2 == 0 and tiles % 4 == 0
+    assert fine // block % 2 == 0
     anywhere = pl.BlockSpec(memory_space=pl.ANY)
     count = local * members
     columns = spread * coarse
@@ -397,7 +389,6 @@
             pltpu.VMEM((DEPTH, levels, PACK // levels, width, fine), jnp.bfloat16),
             pltpu.VMEM((2 * lanes, PACK * width), jnp.bfloat16),
             pltpu.VMEM((2 * per_block, block), jnp.bfloat16),
-            pltpu.VMEM((lanes, fine), jnp.float32),
             pltpu.VMEM((tiles, groups, rows, lanes), jnp.float32),
             pltpu.VMEM((tiles, groups, rows, lanes), jnp.float32),
             pltpu.VMEM((tiles * rows, lanes), jnp.float32),

time: 127 us -> 127 us (level)
  no operation moved by 1% of the time
where the time goes in v3:
time: 127 us; the launch traced here: 126 us
  Pallas kernels  126 us (99%)
    pallas_call x1, Pallas kernels, body(): pl.pallas_call(functools.partial(exchange_kernel, members, tiles, block),...  123 us

profile of v3, /device:TPU:1, one launch (start us, length us, event | category | flops | bytes accessed | tf_op | source)
XLA Modules:
  0.0 126.5 jit_solution(10552416551777251214)
XLA Ops:
  0.0 1.0 select_maximum_fusion.op_ref
  1.0 123.2 %restrict_exchange.1 = (f32[4,80,32,128]{3,2,1,0:T(8,128)S(1)}, f32[4,32,128]{2,1,0:T(8,128)S(1)}) custom-call(bf16[4,40,48,1536]{3,2,1,0:T(8,128)(2,1)} %x_ref.1, f32[400,128]{1,0:T(8,128)S(1)} %select_maximum_fusion.op_ref), custom_call_target="tpu_custom_call" | custom-call | tf_op jit(solution)/shard_map/restrict_exchange/pallas_call | solution.py:380
  124.1 2.4 %center_scale.1 = f32[4,80,32,128]{3,2,1,0:T(8,128)} custom-call(f32[4,80,32,128]{3,2,1,0:T(8,128)S(1)} %get-tuple-element.7.raw_ref, f32[4,32,128]{2,1,0:T(8,128)S(1)} %get-tuple-element.8.mean_ref), custom_call_target="tpu_custom_call" | custom-call | tf_op jit(solution)/shard_map/center_scale/pallas_call | solution.py:408
